TPU v7x, 32 devices: a whole 2x2x4 slice. The times are simulated.
32 devices in a mesh: dp: 2 (over y), expert: 16 (over z, x, core).
Axes of the slice: x: 2, y: 2, z: 4, core: 2. Of those that a mesh axis runs over, the one named last changes fastest.
Arguments:
- tokens: bfloat16 [4096, 2048], P(('dp', 'expert')), may hold values from -6 to 6
- routes: int32 [4096, 2], P(('dp', 'expert')), may hold values from 0 to 15, all different within a row; in each aligned block of 128 rows (0 to 127, 128 to 255, ...) at most 24 rows name the same one
- gates: float32 [4096, 2], P(('dp', 'expert')), may hold values from 0.05 to 1
- grad_out: bfloat16 [4096, 2048], P(('dp', 'expert')), may hold values from -6 to 6
- w_gate: bfloat16 [16, 2048, 768], P('expert', 'dp'), may hold values from -0.125 to 0.125
- w_up: bfloat16 [16, 2048, 768], P('expert', 'dp'), may hold values from -0.125 to 0.125
- w_down: bfloat16 [16, 768, 2048], P('expert', None, 'dp'), may hold values from -0.21875 to 0.21875
Outputs:
- grad_tokens: bfloat16 [4096, 2048], P(('dp', 'expert'))
- grad_gates: float32 [4096, 2], P(('dp', 'expert'))
- grad_down: float32 [16, 768, 2048], P('expert', None, 'dp')
Inputs may be any that keep to these rules, and one draw needn't show every extreme that they name: Within the rows of one device no expert is named by more than 24 routes, a bound that some block reaches; the 2 experts of a token differ.
All inputs are finite; a program needn't handle non-finite values.
Results may differ from a plain program's by a relative error of at most 0.015.
Values may be sent and summed in bfloat16 or wider, within the bound.
No kernel may reach another device: no remote copies, remote signals or barrier semaphores. Data moves between devices by JAX's collectives and lax.ppermute only.
A program may use at most 128 MiB of HBM per device.

v0:
```python
import functools

import jax
import jax.numpy as jnp
from jax import lax
from jax.experimental import pallas as pl
from jax.experimental.pallas import tpu as pltpu
from jax.sharding import PartitionSpec as P

LANES = 128
VMEM_BYTES = 24 * 1024 * 1024
READY_COST_US = 30
TOKENS_COST_US = 30


def contract_last(left, right):
    return lax.dot_general(
        left, right, (((1,), (1,)), ((), ())), preferred_element_type=jnp.float32
    )


def contract_first(left, right):
    return lax.dot_general(
        left, right, (((0,), (0,)), ((), ())), preferred_element_type=jnp.float32
    )


def tile_of(extent, most):
    return most if extent % most == 0 else extent


def slot_positions(routes, experts, stride, base):
    top, count = routes.shape
    labels = lax.broadcasted_iota(jnp.int32, (experts, count), 0)
    named = [labels == routes[k : k + 1, :] for k in range(top)]
    marks = sum(jnp.where(m, 1.0, 0.0) for m in named)
    earlier = lax.broadcasted_iota(jnp.int32, (count, count), 0) < lax.broadcasted_iota(
        jnp.int32, (count, count), 1
    )
    rank = jnp.dot(
        marks.astype(jnp.bfloat16),
        jnp.where(earlier, 1.0, 0.0).astype(jnp.bfloat16),
        preferred_element_type=jnp.float32,
    )
    slot = rank + (labels * stride + base + 1).astype(jnp.float32)
    return [
        jnp.sum(jnp.where(m, slot, 0.0), axis=0, keepdims=True).astype(jnp.int32) - 1
        for m in named
    ]


def by_half(value, cap, half, paired):
    count, width = value.shape
    if paired:
        value = value.reshape(count // (2 * cap), 2, cap, width)
        own, other = value[:, 0], value[:, 1]
    else:
        value = value.reshape(2, count // (2 * cap), cap, width)
        own, other = value[0], value[1]
    first = jnp.where(half == 0, own, other)
    second = jnp.where(half == 0, other, own)
    return jnp.stack([first, second], axis=0 if paired else 1).reshape(count, width)


def dispatch_tokens(experts, cap, place_ref, *refs):
    routes_refs, tokens_refs, (out_ref, pos_ref, pick_ref) = refs[:2], refs[2:4], refs[4:]
    count = tokens_refs[0].shape[0]

    @pl.when(pl.program_id(0) == 0)
    def _():
        rows = lax.broadcasted_iota(jnp.int32, (pick_ref.shape[0], count), 0)
        for c, ref in enumerate(routes_refs):
            near = ref[...] - place_ref[1] * (experts // 2)
            pos = slot_positions(near, experts // 2, 2 * cap, c * cap)
            pick_ref[:, c * count : (c + 1) * count] = sum(
                jnp.where(rows == p, 1.0, 0.0) for p in pos
            ).astype(jnp.bfloat16)
        for k, p in enumerate(slot_positions(routes_refs[0][...], experts, cap, 0)):
            pos_ref[k : k + 1, :] = p

    values = jnp.concatenate([ref[...] for ref in tokens_refs], axis=0)
    out_ref[...] = jnp.dot(
        pick_ref[...], values, preferred_element_type=jnp.float32
    ).astype(out_ref.dtype)


def dispatch_scaled(experts, cap, groups, place_ref, *refs):
    routes_refs, gate_refs = refs[:groups], refs[groups : 2 * groups]
    grad_refs, (out_ref, pick_ref, scale_ref) = refs[2 * groups : 3 * groups], refs[3 * groups :]
    count = grad_refs[0].shape[0]
    slots = out_ref.shape[0]

    @pl.when(pl.program_id(0) == 0)
    def _():
        rows = lax.broadcasted_iota(jnp.int32, (slots, count), 0)
        total = jnp.zeros((slots, 1), jnp.float32)
        for q in range(groups):
            pos = slot_positions(routes_refs[q][...], experts, groups * cap, q * cap)
            hit = jnp.zeros((slots, count), jnp.float32)
            weight = jnp.zeros((slots, count), jnp.float32)
            for k, p in enumerate(pos):
                here = rows == p
                hit = hit + jnp.where(here, 1.0, 0.0)
                weight = weight + jnp.where(here, gate_refs[q][k : k + 1, :], 0.0)
            pick_ref[:, q * count : (q + 1) * count] = hit.astype(jnp.bfloat16)
            total = total + jnp.sum(weight, axis=1, keepdims=True)
        scale_ref[...] = jnp.broadcast_to(total, scale_ref.shape)

    grads = jnp.concatenate([ref[...] for ref in grad_refs], axis=0)
    rows = jnp.dot(pick_ref[...], grads, preferred_element_type=jnp.float32)
    out_ref[...] = (scale_ref[:, :1] * rows).astype(out_ref.dtype)


def stack_kernel(pieces, top_ref, bottom_ref, out_ref, held_ref, sems):
    extent = top_ref.shape[0]
    each = extent // pieces
    moves = []
    for i, ref in enumerate((top_ref, bottom_ref)):
        for n in range(pieces):
            to = slice(i * extent + n * each, i * extent + (n + 1) * each)
            number = i * pieces + n
            load = pltpu.make_async_copy(
                ref.at[n * each : (n + 1) * each], held_ref.at[to], sems.at[0, number]
            )
            moves.append(
                (load, pltpu.make_async_copy(held_ref.at[to], out_ref.at[to], sems.at[1, number]))
            )
    for load, _ in moves:
        load.start()
    for load, store in moves:
        load.wait()
        store.start()
    for _, store in moves:
        store.wait()


def ready_kernel(gate_ref, *refs):
    held_ref, sems = refs[-2:]
    half = gate_ref.shape[0] // 2
    copies = [
        pltpu.make_async_copy(
            gate_ref.at[n * half : (n + 1) * half],
            held_ref.at[n * half : (n + 1) * half],
            sems.at[n],
        )
        for n in range(2)
    ]
    for copy in copies:
        copy.start()
    for copy in copies:
        copy.wait()


def back_kernel(groups, cap, place_ref, rows_ref, down_ref, own_ref, *rest):
    others, all_ref = rest[: groups - 1], rest[groups - 1]
    slots, hidden = own_ref.shape
    count, share = rows_ref.shape
    rows = rows_ref[...].astype(jnp.float32).reshape(count // (groups * cap), groups, cap, share)
    for q in range(groups):
        ordered = by_half(rows[:, q].reshape(slots, share), cap, place_ref[1], False)
        all_ref[q * slots : (q + 1) * slots, :] = ordered.astype(all_ref.dtype)
    step = tile_of(hidden, 256)

    @pl.loop(0, hidden // step)
    def _(j):
        cols = pl.ds(pl.multiple_of(j * step, step), step)
        for q, ref in enumerate((own_ref, *others)):
            part = contract_last(all_ref[q * slots : (q + 1) * slots, :], down_ref[cols, :])
            ref[:, cols] = part.astype(ref.dtype)


def forward_kernel(groups, x_ref, gate_ref, back_ref, own_up_ref, *refs):
    others = refs[: groups - 1]
    act_ref, slope_ref, value_ref, hidden_ref, held_ref, kept_ref = refs[groups - 1 : groups + 5]
    gate_sum_ref, up_sum_ref, sems, back_sem = refs[groups + 5 :]
    share, hidden = gate_ref.shape
    step = tile_of(hidden, 256)
    sources = [gate_ref, *[ref.at[:share] for ref in others]]
    sources += [own_up_ref, *[ref.at[share:] for ref in others]]
    spans = [slice(at, at + step) for at in range(0, hidden, step)]

    order = [i for k in range(groups) for i in (k, groups + k)]
    part_rows = share // 2
    stages = [
        [
            pltpu.make_async_copy(
                sources[i].at[n * part_rows : (n + 1) * part_rows],
                held_ref.at[i - 1, n * part_rows : (n + 1) * part_rows],
                sems.at[n, i - 1],
            )
            for n in range(2)
        ]
        for i in order[1:]
    ]
    stages[-1].append(pltpu.make_async_copy(back_ref, kept_ref, back_sem.at[0]))

    def finish(cols):
        pre_gate, pre_up = gate_sum_ref[:, cols], up_sum_ref[:, cols]
        sig = jax.nn.sigmoid(pre_gate)
        act = pre_gate * sig
        hidden_f = act * pre_up
        act_ref[:, cols] = act
        slope_ref[:, cols] = pre_up * (sig * (1.0 + pre_gate * (1.0 - sig)))
        value_ref[:, cols] = hidden_f
        hidden_ref[:, cols] = hidden_f.astype(hidden_ref.dtype)

    ahead = 2
    for copies in stages[:ahead]:
        for copy in copies:
            copy.start()
    complete = None
    for at, i in enumerate(order):
        k = i % groups
        if at > 0:
            for copy in stages[at - 1]:
                copy.wait()
            if at - 1 + ahead < len(stages):
                for copy in stages[at - 1 + ahead]:
                    copy.start()
        sum_ref = gate_sum_ref if i < groups else up_sum_ref
        for cols in spans:
            part = jnp.dot(
                x_ref[:, k * share : (k + 1) * share],
                gate_ref[:, cols] if i == 0 else held_ref[i - 1, :, cols],
                preferred_element_type=jnp.float32,
            )
            if complete is not None:
                finish(complete)
            sum_ref[:, cols] = part if k == 0 else sum_ref[:, cols] + part
            complete = cols if i == order[-1] else None
    finish(complete)


def backward_kernel(
    groups, cap, half_ref, act_ref, slope_ref, value_ref, gate_ref, held_ref, *refs
):
    parts, (out_ref, d_gate_ref, d_up_ref, rows_ref, out_sems) = refs[:groups], refs[groups:]
    share = held_ref.shape[1]
    width = groups * share
    block = tile_of(share, 512)
    half = half_ref[0]
    back = sum(part[...].astype(jnp.float32) for part in parts)
    score = jnp.sum(back * value_ref[...], axis=1, keepdims=True)
    d_gate_ref[...] = by_half(back * slope_ref[...], cap, half, True).astype(jnp.bfloat16)
    d_up_ref[...] = by_half(back * act_ref[...], cap, half, True).astype(jnp.bfloat16)
    score = by_half(jnp.broadcast_to(score, (score.shape[0], LANES)), cap, half, True)
    rows_ref[:, width:] = score.astype(rows_ref.dtype)
    outs = []

    def send(cols):
        copy = pltpu.make_async_copy(
            rows_ref.at[:, cols], out_ref.at[:, cols], out_sems.at[len(outs)]
        )
        copy.start()
        outs.append(copy)

    send(slice(width, width + LANES))
    for k in range(groups):
        for at in range(0, share, block):
            cols = slice(k * share + at, k * share + at + block)
            gate = gate_ref[at : at + block] if k == 0 else held_ref[k - 1, at : at + block]
            grad = contract_last(d_gate_ref[...], gate)
            grad += contract_last(d_up_ref[...], held_ref[groups - 1 + k, at : at + block])
            rows_ref[:, cols] = grad.astype(rows_ref.dtype)
            send(cols)
    for copy in outs:
        copy.wait()


def combine_kernel(groups, place_ref, pos_ref, gate_ref, rows_ref, tokens_ref, gates_ref):
    top, count = pos_ref.shape
    slots = rows_ref.shape[0]
    width = tokens_ref.shape[1]
    share = width // groups
    places = lax.broadcasted_iota(jnp.int32, (slots, count), 0)
    picks = [
        jnp.where(places == pos_ref[k : k + 1, :], 1.0, 0.0).astype(jnp.bfloat16)
        for k in range(top)
    ]
    both = sum(picks)
    for k in range(groups):
        at = lax.rem(place_ref[0] - k + groups, groups) * share
        tokens_ref[:, pl.ds(pl.multiple_of(at, share), share)] = contract_first(
            both, rows_ref[:, k * share : (k + 1) * share]
        ).astype(tokens_ref.dtype)
    for k in range(top):
        score = contract_first(rows_ref[:, width:], picks[k])
        gates_ref[k : k + 1, :] = score[:1, :] / gate_ref[k : k + 1, :]


def per_device(tokens, routes, gates, grad_out, w_gate, w_up, w_down):
    experts = lax.axis_size("expert")
    groups = lax.axis_size("dp")
    group = lax.axis_index("dp")
    count, width = tokens.shape
    top = routes.shape[1]
    cap = 3 * count * top // (2 * experts)
    slots = experts * cap
    share = width // groups
    hidden = w_gate.shape[2]
    params = pltpu.CompilerParams(vmem_limit_bytes=VMEM_BYTES)
    half = lax.div(lax.axis_index("expert"), experts // 2)
    place = jnp.stack([group, half]).astype(jnp.int32)
    place_group, place_half = group.reshape(1), half.reshape(1)
    halves = [list(range(experts // 2)), list(range(experts // 2, experts))]

    def shifted(value, by):
        return lax.ppermute(value, "dp", [(i, (i + by) % groups) for i in range(groups)])

    def across(value):
        pairs = [(i, (i + experts // 2) % experts) for i in range(experts)]
        return lax.ppermute(value, "expert", pairs)

    def exchanged(rows, among=None):
        count = experts if among is None else len(among[0])
        split = rows.reshape(count, rows.shape[0] // count, rows.shape[1])
        moved = lax.all_to_all(
            split, "expert", split_axis=0, concat_axis=0, axis_index_groups=among, tiled=True
        )
        return moved.reshape(rows.shape)

    def in_hbm(value):
        return pltpu.with_memory_space_constraint(value, pltpu.HBM)

    routes_t, gates_t = jnp.transpose(routes), jnp.transpose(gates)
    routes_all = [routes_t] + [shifted(routes_t, k) for k in range(1, groups)]
    gates_all = [gates_t] + [shifted(gates_t, k) for k in range(1, groups)]
    grads = [
        shifted(
            lax.dynamic_slice(grad_out, (0, lax.rem(group + k, groups) * share), (count, share)), k
        )
        for k in range(1, groups)
    ]
    any_spec = pl.BlockSpec(memory_space=pl.ANY)
    both = pl.pallas_call(
        functools.partial(stack_kernel, 4),
        out_shape=pltpu.HBM((2 * share, hidden), jnp.bfloat16),
        in_specs=[any_spec] * 2,
        out_specs=any_spec,
        scratch_shapes=[
            pltpu.VMEM((2 * share, hidden), jnp.bfloat16),
            pltpu.SemaphoreType.DMA((2, 8)),
        ],
        compiler_params=params,
        name="stack",
    )(in_hbm(w_gate[0]), in_hbm(w_up[0]))
    both, gates_own = lax.optimization_barrier((both, gates_t))
    both, grads, routes_all, gates_all = lax.optimization_barrier(
        (both, grads, routes_all, gates_all)
    )
    routes_across = across(routes_t)
    tokens_sent, routes_across = lax.optimization_barrier((tokens, routes_across))
    tokens_across = across(tokens_sent)
    weights_moved = [shifted(both, k) for k in range(1, groups)]

    block = tile_of(share, 512)
    steps = share // block
    small_spec = pl.BlockSpec((top, count), lambda c, g: (0, 0))
    scaled = pl.pallas_call(
        functools.partial(dispatch_scaled, experts, cap, groups),
        out_shape=pltpu.HBM((groups * slots, share), jnp.bfloat16),
        grid_spec=pltpu.PrefetchScalarGridSpec(
            num_scalar_prefetch=1,
            grid=(steps,),
            in_specs=[small_spec] * (2 * groups)
            + [pl.BlockSpec((count, block), lambda c, g: (0, g[0] * steps + c))]
            + [pl.BlockSpec((count, block), lambda c, g: (0, c))] * (groups - 1),
            out_specs=pl.BlockSpec((groups * slots, block), lambda c, g: (0, c)),
            scratch_shapes=[
                pltpu.VMEM((groups * slots, groups * count), jnp.bfloat16),
                pltpu.VMEM((groups * slots, LANES), jnp.float32),
            ],
        ),
        compiler_params=params,
        name="dispatch_scaled",
    )(
        place_group,
        in_hbm(routes_t),
        *routes_all[1:],
        in_hbm(gates_own),
        *gates_all[1:],
        in_hbm(grad_out),
        *grads,
    )
    scaled_rows = exchanged(scaled)

    sent, pos = pl.pallas_call(
        functools.partial(dispatch_tokens, experts, cap),
        out_shape=(
            pltpu.HBM((slots, width), jnp.bfloat16),
            jax.ShapeDtypeStruct((top, count), jnp.int32),
        ),
        grid_spec=pltpu.PrefetchScalarGridSpec(
            num_scalar_prefetch=1,
            grid=(groups,),
            in_specs=[small_spec] * 2
            + [
                pl.BlockSpec(
                    (count, share), lambda k, g: (0, lax.rem(g[0] - k + groups, groups))
                )
            ]
            * 2,
            out_specs=(pl.BlockSpec((slots, share), lambda k, g: (0, k)), small_spec),
            scratch_shapes=[pltpu.VMEM((slots, 2 * count), jnp.bfloat16)],
        ),
        cost_estimate=pl.CostEstimate(
            flops=TOKENS_COST_US * 10**9, bytes_accessed=TOKENS_COST_US * 10**6, transcendentals=0
        ),
        compiler_params=params,
        name="dispatch_tokens",
    )(place, in_hbm(routes_t), routes_across, in_hbm(tokens), in_hbm(tokens_across))
    x_rows = exchanged(sent, halves)

    whole_spec = pl.BlockSpec(memory_space=pltpu.VMEM)
    *weights_moved, gate_held = pl.pallas_call(
        ready_kernel,
        out_shape=[pltpu.HBM(value.shape, value.dtype) for value in weights_moved]
        + [pltpu.VMEM((share, hidden), jnp.bfloat16)],
        in_specs=[any_spec] * groups,
        out_specs=[any_spec] * (groups - 1) + [whole_spec],
        input_output_aliases={k + 1: k for k in range(groups - 1)},
        scratch_shapes=[pltpu.SemaphoreType.DMA((2,))],
        cost_estimate=pl.CostEstimate(
            flops=READY_COST_US * 10**9, bytes_accessed=READY_COST_US * 10**6, transcendentals=0
        ),
        compiler_params=params,
        name="ready",
    )(in_hbm(w_gate[0]), *[in_hbm(value) for value in weights_moved])

    place_spec = pl.BlockSpec(memory_space=pltpu.SMEM)

    back_own, *rest = pl.pallas_call(
        functools.partial(back_kernel, groups, cap),
        out_shape=[pltpu.HBM((slots, hidden), jnp.float32)]
        + [pltpu.HBM((slots, hidden), jnp.bfloat16)] * (groups - 1)
        + [pltpu.HBM((groups * slots, share), jnp.bfloat16)],
        in_specs=[place_spec, pl.BlockSpec(), pl.BlockSpec()],
        compiler_params=params,
        name="back",
    )(place, scaled_rows, in_hbm(w_down[0]))
    scaled_all = rest[-1]
    back_parts = [shifted(rest[k - 1], -k) for k in range(1, groups)]

    *factors, hidden_own, held, back_kept = pl.pallas_call(
        functools.partial(forward_kernel, groups),
        out_shape=[pltpu.VMEM((slots, hidden), jnp.float32)] * 3
        + [
            pltpu.HBM((slots, hidden), jnp.bfloat16),
            pltpu.VMEM((2 * groups - 1, share, hidden), jnp.bfloat16),
            pltpu.VMEM((slots, hidden), jnp.float32),
        ],
        in_specs=[whole_spec] * 2 + [any_spec] * (groups + 1),
        scratch_shapes=[
            pltpu.VMEM((slots, hidden), jnp.float32),
            pltpu.VMEM((slots, hidden), jnp.float32),
            pltpu.SemaphoreType.DMA((2, 2 * groups - 1)),
            pltpu.SemaphoreType.DMA((1,)),
        ],
        compiler_params=params,
        name="forward",
    )(x_rows, gate_held, in_hbm(back_own), in_hbm(w_up[0]), *[in_hbm(w) for w in weights_moved])

    pieces = groups * (share // tile_of(share, 512))
    returning = pl.pallas_call(
        functools.partial(backward_kernel, groups, cap),
        out_shape=pltpu.HBM((slots, width + LANES), jnp.bfloat16),
        in_specs=[place_spec] + [whole_spec] * (5 + groups),
        out_specs=any_spec,
        scratch_shapes=[
            pltpu.VMEM((slots, hidden), jnp.bfloat16),
            pltpu.VMEM((slots, hidden), jnp.bfloat16),
            pltpu.VMEM((slots, width + LANES), jnp.bfloat16),
            pltpu.SemaphoreType.DMA((pieces + 1,)),
        ],
        compiler_params=params,
        name="backward",
    )(place_half, *factors, gate_held, held, back_kept, *back_parts)
    returned = exchanged(returning)

    hiddens = [hidden_own] + [shifted(hidden_own, k) for k in range(1, groups)]
    grad_down = contract_first(jnp.concatenate(hiddens, axis=0), scaled_all)[None]

    grad_tokens, grad_gates = pl.pallas_call(
        functools.partial(combine_kernel, groups),
        out_shape=(
            jax.ShapeDtypeStruct((count, width), jnp.bfloat16),
            jax.ShapeDtypeStruct((top, count), jnp.float32),
        ),
        in_specs=[pl.BlockSpec(memory_space=pltpu.SMEM)] + [whole_spec] * 3,
        compiler_params=params,
        name="combine",
    )(place_group, pos, gates_t, returned)
    return (grad_tokens, jnp.transpose(grad_gates), grad_down)


def solution(mesh):
    placed = (
        P(("dp", "expert"), None),
        P(("dp", "expert"), None),
        P(("dp", "expert"), None),
        P(("dp", "expert"), None),
        P("expert", "dp", None),
        P("expert", "dp", None),
        P("expert", None, "dp"),
    )
    return jax.shard_map(
        per_device,
        mesh=mesh,
        in_specs=placed,
        out_specs=(P(("dp", "expert"), None), P(("dp", "expert"), None), P("expert", None, "dp")),
        check_vma=False,
    )
```

profile of v0, /device:TPU:11, one launch (start us, length us, event | category | flops | bytes accessed | tf_op | source)
XLA Modules:
  0.0 146.6 jit_solution(6293343216184571608)
XLA Ops:
  0.6 1.0 constant_dynamic-slice_fusion
  1.6 1.3 collective-permute-start.2
  2.9 2.3 %collective-permute-start = (s32[2,128]{1,0:T(2,128)}, s32[2,128]{1,0:T(2,128)S(1)}, u32[]{:S(2)}, u32[]{:S(2)}) collective-permute-start(s32[2,128]{1,0:T(2,128)} %bitcast.31), channel_id=1, source_target_pairs={{0,8},{1,9},{2,10},{3,11},{4,12},{5,13},{6,14},{7,15},{8,0},{9,1},... | collective-permute-start | bytes 3080 | tf_op jit(solution)/shard_map/ppermute | solution.py:312
  5.2 1.2 collective-permute-done.refs_1_
  6.5 2.3 %collective-permute-start.1 = (bf16[128,2048]{1,0:T(8,128)(2,1)}, bf16[128,2048]{1,0:T(8,128)(2,1)S(1)}, u32[]{:S(2)}, u32[]{:S(2)}) collective-permute-start(bf16[128,2048]{1,0:T(8,128)(2,1)} %refs_2_.1), channel_id=1, source_target_pairs={{0,8},{1,9},{2,10},{3,11},{4,12},{5,13},{6,14},{7,15},{8,0},{9,1},... | collective-permute-start | bytes 1572872 | tf_op jit(solution)/shard_map/ppermute | solution.py:312
  8.8 0.2 collective-permute-start.3
  9.0 1.2 collective-permute-start.4
  10.2 2.8 %stack.10 = bf16[2048,768]{1,0:T(8,128)(2,1)} custom-call(bf16[1024,768]{1,0:T(8,128)(2,1)} %bitcast.29, bf16[1024,768]{1,0:T(8,128)(2,1)} %bitcast.25), custom_call_target="tpu_custom_call" | custom-call | tf_op jit(solution)/shard_map/stack/pallas_call | solution.py:335
  13.0 0.0 collective-permute-done.3.refs_1_
  13.0 0.0 collective-permute-done.4.refs_3_
  13.1 0.3 collective-permute-start.5
  13.3 3.1 %dispatch_scaled.1 = bf16[768,1024]{1,0:T(8,128)(2,1)} custom-call(s32[1]{0:T(128)} %bitcast.place_ref, s32[2,128]{1,0:T(2,128)} %bitcast.33, s32[2,128]{1,0:T(2,128)S(1)} %collective-permute-done.3.refs_1_, f32[2,128]{1,0:T(2,128)} %bitcast.21, f32[2,128]{1,0:T(2,128)S(1)} %collective-permute-done.4.refs_3_, bf16[128,2048]{1,0:T(8,128)(2,1)} %refs_4_.1, ...), custom_call_target="tpu_custom_call" | custom-call | tf_op jit(solution)/shard_map/dispatch_scaled/pallas_call | solution.py:359
  16.5 7.5 %all-to-all-start.1 = ((bf16[16,48,1024]{2,1,0:T(8,128)(2,1)}), bf16[16,48,1024]{2,1,0:T(8,128)(2,1)S(1)}, u32[]{:S(2)}, u32[]{:S(2)}) async-start(bf16[16,48,1024]{2,1,0:T(8,128)(2,1)} %bitcast.24), calls=%async_computation.1 | async-start | bytes 3145728 | tf_op jit(solution)/shard_map/all_to_all | solution.py:317
  23.9 0.1 pad_add_fusion.place_ref
  24.0 24.4 %collective-permute-done.1.refs_3_ = bf16[128,2048]{1,0:T(8,128)(2,1)S(1)} collective-permute-done((bf16[128,2048]{1,0:T(8,128)(2,1)}, bf16[128,2048]{1,0:T(8,128)(2,1)S(1)}, u32[]{:S(2)}, u32[]{:S(2)}) %collective-permute-start.1) | collective-permute-done | bytes 524320 | tf_op jit(solution)/shard_map/ppermute | solution.py:312
  48.5 0.8 copy-done.2
  49.3 3.6 %dispatch_tokens.1 = (bf16[384,2048]{1,0:T(8,128)(2,1)}, s32[2,128]{1,0:T(2,128)S(1)}) custom-call(s32[2]{0:T(128)S(1)} %pad_add_fusion.place_ref, s32[2,128]{1,0:T(2,128)} %bitcast.34, s32[2,128]{1,0:T(2,128)S(1)} %collective-permute-done.refs_1_, bf16[128,2048]{1,0:T(8,128)(2,1)} %refs_2_.1, bf16[128,2048]{1,0:T(8,128)(2,1)} %copy-done.2), custom_call_target="tpu_custom_call" | custom-call | flops 30000001024 | bytes 30000000 | tf_op jit(solution)/shard_map/dispatch_tokens/pallas_call | solution.py:387
  52.9 12.7 %all-to-all-done.1 = bf16[16,48,1024]{2,1,0:T(8,128)(2,1)S(1)} async-done(((bf16[16,48,1024]{2,1,0:T(8,128)(2,1)}), bf16[16,48,1024]{2,1,0:T(8,128)(2,1)S(1)}, u32[]{:S(2)}, u32[]{:S(2)}) %all-to-all-start.1) | async-done | bytes 1572896 | tf_op jit(solution)/shard_map/all_to_all | solution.py:317
  65.6 4.3 %all-to-all-start = ((bf16[8,48,2048]{2,1,0:T(8,128)(2,1)}), bf16[8,48,2048]{2,1,0:T(8,128)(2,1)S(1)}, u32[]{:S(2)}, u32[]{:S(2)}) async-start(bf16[8,48,2048]{2,1,0:T(8,128)(2,1)} %bitcast.27), calls=%async_computation | async-start | bytes 3145728 | tf_op jit(solution)/shard_map/all_to_all | solution.py:317
  69.9 5.2 %back.1 = (f32[384,768]{1,0:T(8,128)}, bf16[384,768]{1,0:T(8,128)(2,1)}, bf16[768,1024]{1,0:T(8,128)(2,1)}) custom-call(s32[2]{0:T(128)S(1)} %pad_add_fusion.place_ref, bf16[768,1024]{1,0:T(8,128)(2,1)S(1)} %bitcast.18, bf16[768,1024]{1,0:T(8,128)(2,1)} %bitcast.28), custom_call_target="tpu_custom_call" | custom-call | tf_op jit(solution)/shard_map/back/pallas_call | solution.py:432
  75.2 0.2 collective-permute-start.6
  75.4 4.7 %collective-permute-done.5.refs_0_ = bf16[2048,768]{1,0:T(8,128)(2,1)} collective-permute-done((bf16[2048,768]{1,0:T(8,128)(2,1)}, bf16[2048,768]{1,0:T(8,128)(2,1)}, u32[]{:S(2)}, u32[]{:S(2)}) %collective-permute-start.5) | collective-permute-done | bytes 3145760 | tf_op jit(solution)/shard_map/ppermute | solution.py:308
  80.1 1.4 ready.1
  81.5 6.7 %all-to-all-done = bf16[8,48,2048]{2,1,0:T(8,128)(2,1)S(1)} async-done(((bf16[8,48,2048]{2,1,0:T(8,128)(2,1)}), bf16[8,48,2048]{2,1,0:T(8,128)(2,1)S(1)}, u32[]{:S(2)}, u32[]{:S(2)}) %all-to-all-start) | async-done | bytes 1572896 | tf_op jit(solution)/shard_map/all_to_all | solution.py:317
  88.2 5.9 %forward.1 = (f32[384,768]{1,0:T(8,128)S(1)}, f32[384,768]{1,0:T(8,128)S(1)}, f32[384,768]{1,0:T(8,128)S(1)}, bf16[384,768]{1,0:T(8,128)(2,1)}, bf16[3,1024,768]...) custom-call(bf16[384,2048]{1,0:T(8,128)(2,1)S(1)} %bitcast.19, bf16[1024,768]{1,0:T(8,128)(2,1)S(1)} %get-tuple-element.32.gate_ref, ...), custom_call_target="tpu_custom_call" | custom-call | tf_op jit(solution)/shard_map/forward/pallas_call | solution.py:444
  94.1 4.7 %backward.1 = bf16[384,2176]{1,0:T(8,128)(2,1)} custom-call(s32[1]{0:T(128)} %bitcast.1.half_ref, f32[384,768]{1,0:T(8,128)S(1)} %get-tuple-element.39.act_ref, f32[384,768]{1,0:T(8,128)S(1)} %get-tuple-element.40.slope_ref, f32[384,768]{1,0:T(8,128)S(1)} %get-tuple-element.41.value_ref, bf16[1024,768]{1,0:T(8,128)(2,1)S(1)} %get-tuple-element.32.gate_ref, ...), custom_call_target="tpu_custom_call" | custom-call | tf_op jit(solution)/shard_map/backward/pallas_call | solution.py:464
  98.8 8.3 %all-to-all-start.2 = ((bf16[16,24,2176]{2,1,0:T(8,128)(2,1)}), bf16[16,24,2176]{2,1,0:T(8,128)(2,1)S(1)}, u32[]{:S(2)}, u32[]{:S(2)}) async-start(bf16[16,24,2176]{2,1,0:T(8,128)(2,1)} %bitcast.23), calls=%async_computation.2 | async-start | bytes 3342336 | tf_op jit(solution)/shard_map/all_to_all | solution.py:317
  107.0 0.2 collective-permute-start.7
  107.3 14.5 %collective-permute-done.7 = bf16[384,768]{1,0:T(8,128)(2,1)S(1)} collective-permute-done((bf16[384,768]{1,0:T(8,128)(2,1)}, bf16[384,768]{1,0:T(8,128)(2,1)S(1)}, u32[]{:S(2)}, u32[]{:S(2)}) %collective-permute-start.7) | collective-permute-done | bytes 589856 | tf_op jit(solution)/shard_map/ppermute | solution.py:308
  121.8 4.2 %convolution_bitcast_fusion = f32[1,768,1024]{2,1,0:T(8,128)} fusion(bf16[768,1024]{1,0:T(8,128)(2,1)S(1)} %copy-done.1, bf16[384,768]{1,0:T(8,128)(2,1)S(1)} %collective-permute-done.7, bf16[384,768]{1,0:T(8,128)(2,1)} %get-tuple-element.47), kind=kOutput, calls=%fused_computation | convolution fusion | flops 1210318848 | bytes 5898240 | tf_op jit(solution)/shard_map/dot_general | solution.py:23
  126.0 19.3 %all-to-all-done.2 = bf16[16,24,2176]{2,1,0:T(8,128)(2,1)S(1)} async-done(((bf16[16,24,2176]{2,1,0:T(8,128)(2,1)}), bf16[16,24,2176]{2,1,0:T(8,128)(2,1)S(1)}, u32[]{:S(2)}, u32[]{:S(2)}) %all-to-all-start.2) | async-done | bytes 1671200 | tf_op jit(solution)/shard_map/all_to_all | solution.py:317
  145.3 1.3 combine.1
  (7 shorter events, 0.0 us)
Async XLA Ops:
  1.6 11.4 %collective-permute-start.2 = (bf16[128,1024]{1,0:T(8,128)(2,1)S(1)}, bf16[128,1024]{1,0:T(8,128)(2,1)S(1)}, u32[]{:S(2)}, u32[]{:S(2)}) collective-permute-start(bf16[128,1024]{1,0:T(8,128)(2,1)S(1)} %constant_dynamic-slice_fusion), channel_id=1, source_target_pairs={{0,16},{16,0},{1,17},{17,1},{2,18},{18,2},{3,19},{19,3},{4,20},{20... | collective-permute-start | bytes 786440 | tf_op jit(solution)/shard_map/ppermute | solution.py:308
  2.9 3.5 %collective-permute-start = (s32[2,128]{1,0:T(2,128)}, s32[2,128]{1,0:T(2,128)S(1)}, u32[]{:S(2)}, u32[]{:S(2)}) collective-permute-start(s32[2,128]{1,0:T(2,128)} %bitcast.31), channel_id=1, source_target_pairs={{0,8},{1,9},{2,10},{3,11},{4,12},{5,13},{6,14},{7,15},{8,0},{9,1},... | collective-permute-start | bytes 3080 | tf_op jit(solution)/shard_map/ppermute | solution.py:312
  6.5 42.0 %collective-permute-start.1 = (bf16[128,2048]{1,0:T(8,128)(2,1)}, bf16[128,2048]{1,0:T(8,128)(2,1)S(1)}, u32[]{:S(2)}, u32[]{:S(2)}) collective-permute-start(bf16[128,2048]{1,0:T(8,128)(2,1)} %refs_2_.1), channel_id=1, source_target_pairs={{0,8},{1,9},{2,10},{3,11},{4,12},{5,13},{6,14},{7,15},{8,0},{9,1},... | collective-permute-start | bytes 1572872 | tf_op jit(solution)/shard_map/ppermute | solution.py:312
  8.8 4.3 %collective-permute-start.3 = (s32[2,128]{1,0:T(2,128)}, s32[2,128]{1,0:T(2,128)S(1)}, u32[]{:S(2)}, u32[]{:S(2)}) collective-permute-start(s32[2,128]{1,0:T(2,128)} %bitcast.32), channel_id=1, source_target_pairs={{0,16},{16,0},{1,17},{17,1},{2,18},{18,2},{3,19},{19,3},{4,20},{20... | collective-permute-start | bytes 3080 | tf_op jit(solution)/shard_map/ppermute | solution.py:308
  9.0 4.0 %collective-permute-start.4 = (f32[2,128]{1,0:T(2,128)}, f32[2,128]{1,0:T(2,128)S(1)}, u32[]{:S(2)}, u32[]{:S(2)}) collective-permute-start(f32[2,128]{1,0:T(2,128)} %bitcast.20), channel_id=1, source_target_pairs={{0,16},{16,0},{1,17},{17,1},{2,18},{18,2},{3,19},{19,3},{4,20},{20... | collective-permute-start | bytes 3080 | tf_op jit(solution)/shard_map/ppermute | solution.py:308
  13.1 67.0 %collective-permute-start.5 = (bf16[2048,768]{1,0:T(8,128)(2,1)}, bf16[2048,768]{1,0:T(8,128)(2,1)}, u32[]{:S(2)}, u32[]{:S(2)}) collective-permute-start(bf16[2048,768]{1,0:T(8,128)(2,1)} %stack.10), channel_id=1, source_target_pairs={{0,16},{16,0},{1,17},{17,1},{2,18},{18,2},{3,19},{19,3},{4,20},{20... | collective-permute-start | bytes 9437192 | tf_op jit(solution)/shard_map/ppermute | solution.py:308
  16.5 49.2 %all-to-all-start.1 = ((bf16[16,48,1024]{2,1,0:T(8,128)(2,1)}), bf16[16,48,1024]{2,1,0:T(8,128)(2,1)S(1)}, u32[]{:S(2)}, u32[]{:S(2)}) async-start(bf16[16,48,1024]{2,1,0:T(8,128)(2,1)} %bitcast.24), calls=%async_computation.1 | async-start | bytes 3145728 | tf_op jit(solution)/shard_map/all_to_all | solution.py:317
  48.5 0.8 copy-start.2
  65.6 22.5 %all-to-all-start = ((bf16[8,48,2048]{2,1,0:T(8,128)(2,1)}), bf16[8,48,2048]{2,1,0:T(8,128)(2,1)S(1)}, u32[]{:S(2)}, u32[]{:S(2)}) async-start(bf16[8,48,2048]{2,1,0:T(8,128)(2,1)} %bitcast.27), calls=%async_computation | async-start | bytes 3145728 | tf_op jit(solution)/shard_map/all_to_all | solution.py:317
  75.2 18.9 %collective-permute-start.6 = (bf16[384,768]{1,0:T(8,128)(2,1)}, bf16[384,768]{1,0:T(8,128)(2,1)}, u32[]{:S(2)}, u32[]{:S(2)}) collective-permute-start(bf16[384,768]{1,0:T(8,128)(2,1)} %get-tuple-element.44), channel_id=1, source_target_pairs={{0,16},{16,0},{1,17},{17,1},{2,18},{18,2},{3,19},{19,3},{4,20},{20... | collective-permute-start | bytes 1769480 | tf_op jit(solution)/shard_map/ppermute | solution.py:308
  98.8 23.0 %copy-start.1 = (bf16[768,1024]{1,0:T(8,128)(2,1)S(1)}, bf16[768,1024]{1,0:T(8,128)(2,1)}, u32[]{:S(2)}) copy-start(bf16[768,1024]{1,0:T(8,128)(2,1)} %get-tuple-element.48) | copy-start | bytes 4718596
  98.8 46.5 %all-to-all-start.2 = ((bf16[16,24,2176]{2,1,0:T(8,128)(2,1)}), bf16[16,24,2176]{2,1,0:T(8,128)(2,1)S(1)}, u32[]{:S(2)}, u32[]{:S(2)}) async-start(bf16[16,24,2176]{2,1,0:T(8,128)(2,1)} %bitcast.23), calls=%async_computation.2 | async-start | bytes 3342336 | tf_op jit(solution)/shard_map/all_to_all | solution.py:317
  107.0 14.8 %collective-permute-start.7 = (bf16[384,768]{1,0:T(8,128)(2,1)}, bf16[384,768]{1,0:T(8,128)(2,1)S(1)}, u32[]{:S(2)}, u32[]{:S(2)}) collective-permute-start(bf16[384,768]{1,0:T(8,128)(2,1)} %get-tuple-element.47), channel_id=1, source_target_pairs={{0,16},{16,0},{1,17},{17,1},{2,18},{18,2},{3,19},{19,3},{4,20},{20... | collective-permute-start | bytes 1769480 | tf_op jit(solution)/shard_map/ppermute | solution.py:308
  121.8 23.5 %copy-start = (f32[128,2]{0,1:T(2,128)S(1)}, f32[128,2]{0,1:T(2,128)}, u32[]{:S(2)}) copy-start(f32[128,2]{0,1:T(2,128)} %param.9) | copy-start | bytes 3076
where the time goes:
time: 147 us
  waiting for transfers between devices  83.7 us (57%)
  starting transfers between devices  28.2 us (19%)
  Pallas kernels  28 us (19%)
  matrix products  4.19 us (3%)
  local copies, waits for them, and re-layouts  1.77 us (1%)
    all_to_all x3, waiting for transfers between devices, exchanged(): lax.all_to_all(split, 'expert', split_axis=0, concat_axis=0, axis_index_g...  38.8 us
    ppermute x2, waiting for transfers between devices, across(): return lax.ppermute(value, 'expert', pairs)  25.7 us
    all_to_all x3, starting transfers between devices, exchanged(): lax.all_to_all(split, 'expert', split_axis=0, concat_axis=0, axis_index_g...  20 us
    ppermute x6, waiting for transfers between devices, shifted(): lax.ppermute(value, 'dp', [(i, (i + by) % groups) for i in range(groups)])  19.2 us
    pallas_call x1, Pallas kernels, per_device(): pl.pallas_call(functools.partial(forward_kernel, groups), out_shape=[pltp...  5.88 us
    pallas_call x1, Pallas kernels, per_device(): pl.pallas_call(functools.partial(back_kernel, groups, cap), out_shape=[pl...  5.23 us
    pallas_call x1, Pallas kernels, per_device(): pl.pallas_call(functools.partial(backward_kernel, groups, cap), out_shape...  4.72 us
    ppermute x2, starting transfers between devices, across(): return lax.ppermute(value, 'expert', pairs)  4.62 us
  transfers between devices with their start and end apart: 11, of which 7 were waited for; matrix products, arithmetic and copies ran while one was open for 3% of the time, Pallas kernels for 15%

commit v1 on v0

--- a/solution.py
+++ b/solution.py
@@ -234,12 +234,30 @@
 def backward_kernel(
     groups, cap, half_ref, act_ref, slope_ref, value_ref, gate_ref, held_ref, *refs
 ):
-    parts, (out_ref, d_gate_ref, d_up_ref, rows_ref, out_sems) = refs[:groups], refs[groups:]
+    kept_ref, others = refs[0], refs[1:groups]
+    out_ref, d_gate_ref, d_up_ref, rows_ref, other_ref, out_sems, other_sems = refs[groups:]
     share = held_ref.shape[1]
     width = groups * share
     block = tile_of(share, 512)
     half = half_ref[0]
-    back = sum(part[...].astype(jnp.float32) for part in parts)
+    pieces = other_sems.shape[1]
+    each = kept_ref.shape[0] // pieces
+    copies = [
+        pltpu.make_async_copy(
+            ref.at[n * each : (n + 1) * each],
+            other_ref.at[k, n * each : (n + 1) * each],
+            other_sems.at[k, n],
+        )
+        for k, ref in enumerate(others)
+        for n in range(pieces)
+    ]
+    for copy in copies:
+        copy.start()
+    for copy in copies:
+        copy.wait()
+    back = kept_ref[...]
+    for k in range(groups - 1):
+        back += other_ref[k].astype(jnp.float32)
     score = jnp.sum(back * value_ref[...], axis=1, keepdims=True)
     d_gate_ref[...] = by_half(back * slope_ref[...], cap, half, True).astype(jnp.bfloat16)
     d_up_ref[...] = by_half(back * act_ref[...], cap, half, True).astype(jnp.bfloat16)
@@ -345,15 +363,15 @@
         name="stack",
     )(in_hbm(w_gate[0]), in_hbm(w_up[0]))
     both, gates_own = lax.optimization_barrier((both, gates_t))
+    routes_across = across(routes_t)
+    tokens_sent, routes_across, both = lax.optimization_barrier((tokens, routes_across, both))
+    tokens_across = across(tokens_sent)
     both, grads, routes_all, gates_all = lax.optimization_barrier(
         (both, grads, routes_all, gates_all)
     )
-    routes_across = across(routes_t)
-    tokens_sent, routes_across = lax.optimization_barrier((tokens, routes_across))
-    tokens_across = across(tokens_sent)
     weights_moved = [shifted(both, k) for k in range(1, groups)]
 
-    block = tile_of(share, 512)
+    block = tile_of(share, 256)
     steps = share // block
     small_spec = pl.BlockSpec((top, count), lambda c, g: (0, 0))
     scaled = pl.pallas_call(
@@ -464,17 +482,19 @@
     returning = pl.pallas_call(
         functools.partial(backward_kernel, groups, cap),
         out_shape=pltpu.HBM((slots, width + LANES), jnp.bfloat16),
-        in_specs=[place_spec] + [whole_spec] * (5 + groups),
+        in_specs=[place_spec] + [whole_spec] * 6 + [any_spec] * (groups - 1),
         out_specs=any_spec,
         scratch_shapes=[
             pltpu.VMEM((slots, hidden), jnp.bfloat16),
             pltpu.VMEM((slots, hidden), jnp.bfloat16),
             pltpu.VMEM((slots, width + LANES), jnp.bfloat16),
+            pltpu.VMEM((groups - 1, slots, hidden), jnp.bfloat16),
             pltpu.SemaphoreType.DMA((pieces + 1,)),
+            pltpu.SemaphoreType.DMA((groups - 1, 4)),
         ],
         compiler_params=params,
         name="backward",
-    )(place_half, *factors, gate_held, held, back_kept, *back_parts)
+    )(place_half, *factors, gate_held, held, back_kept, *[in_hbm(p) for p in back_parts])
     returned = exchanged(returning)
 
     hiddens = [hidden_own] + [shifted(hidden_own, k) for k in range(1, groups)]

time: 147 us -> 147 us (level)
    all_to_all x3, waiting for transfers between devices: 38.8 us -> 52.4 us  [exchanged(): lax.all_to_all(split, 'expert', split_axis=0, concat_axis=0, axis_index_g...]
    ppermute x2, waiting for transfers between devices: 25.7 us -> 14.3 us  [across(): return lax.ppermute(value, 'expert', pairs)]
    ppermute x6, waiting for transfers between devices: 19.2 us -> 16.7 us  [shifted(): lax.ppermute(value, 'dp', [(i, (i + by) % groups) for i in range(groups)])]
    ppermute x2, starting transfers between devices: 4.62 us -> 2.96 us  [across(): return lax.ppermute(value, 'expert', pairs)]
  transfers between devices with their start and end apart: 11 -> 11, of which waited for: 7 -> 8; matrix products, arithmetic and copies ran while one was open for 3% -> 3% of each run, Pallas kernels for 15% -> 16%
where the time goes in v1:
time: 147 us; the launch traced here: 146 us
  waiting for transfers between devices  83.4 us (57%)
  Pallas kernels  29.4 us (20%)
  starting transfers between devices  26.8 us (18%)
  matrix products  4.19 us (3%)
  local copies, waits for them, and re-layouts  1.78 us (1%)
    all_to_all x3, waiting for transfers between devices, exchanged(): lax.all_to_all(split, 'expert', split_axis=0, concat_axis=0, axis_index_g...  52.4 us
    all_to_all x3, starting transfers between devices, exchanged(): lax.all_to_all(split, 'expert', split_axis=0, concat_axis=0, axis_index_g...  19.4 us
    ppermute x6, waiting for transfers between devices, shifted(): lax.ppermute(value, 'dp', [(i, (i + by) % groups) for i in range(groups)])  16.7 us
    ppermute x2, waiting for transfers between devices, across(): return lax.ppermute(value, 'expert', pairs)  14.3 us
    pallas_call x1, Pallas kernels, per_device(): pl.pallas_call(functools.partial(forward_kernel, groups), out_shape=[pltp...  5.87 us
    pallas_call x1, Pallas kernels, per_device(): pl.pallas_call(functools.partial(back_kernel, groups, cap), out_shape=[pl...  5.26 us
    pallas_call x1, Pallas kernels, per_device(): pl.pallas_call(functools.partial(backward_kernel, groups, cap), out_shape...  4.77 us
    ppermute x6, starting transfers between devices, shifted(): lax.ppermute(value, 'dp', [(i, (i + by) % groups) for i in range(groups)])  4.46 us
  transfers between devices with their start and end apart: 11, of which 8 were waited for; matrix products, arithmetic and copies ran while one was open for 3% of the time, Pallas kernels for 16%

profile of v1, /device:TPU:11, one launch (start us, length us, event | category | flops | bytes accessed | tf_op | source)
XLA Modules:
  0.0 146.5 jit_solution(12251654862226087677)
XLA Ops:
  0.6 1.0 constant_dynamic-slice_fusion
  1.6 1.3 collective-permute-start.2
  2.9 2.3 %collective-permute-start = (s32[2,128]{1,0:T(2,128)}, s32[2,128]{1,0:T(2,128)S(1)}, u32[]{:S(2)}, u32[]{:S(2)}) collective-permute-start(s32[2,128]{1,0:T(2,128)} %bitcast.31), channel_id=1, source_target_pairs={{0,8},{1,9},{2,10},{3,11},{4,12},{5,13},{6,14},{7,15},{8,0},{9,1},... | collective-permute-start | bytes 3080 | tf_op jit(solution)/shard_map/ppermute | solution.py:330
  5.2 2.8 %stack.10 = bf16[2048,768]{1,0:T(8,128)(2,1)} custom-call(bf16[1024,768]{1,0:T(8,128)(2,1)} %bitcast.29, bf16[1024,768]{1,0:T(8,128)(2,1)} %bitcast.25), custom_call_target="tpu_custom_call" | custom-call | tf_op jit(solution)/shard_map/stack/pallas_call | solution.py:353
  8.1 0.0 collective-permute-done.refs_1_
  8.1 0.7 collective-permute-start.1
  8.8 0.2 collective-permute-start.3
  9.0 1.2 collective-permute-start.4
  10.2 0.9 collective-permute-done.3.refs_1_
  11.2 0.2 collective-permute-done.4.refs_3_
  11.4 1.2 collective-permute-start.5
  12.7 4.4 %dispatch_scaled.1 = bf16[768,1024]{1,0:T(8,128)(2,1)} custom-call(s32[1]{0:T(128)} %bitcast.place_ref, s32[2,128]{1,0:T(2,128)} %bitcast.32, s32[2,128]{1,0:T(2,128)S(1)} %collective-permute-done.3.refs_1_, f32[2,128]{1,0:T(2,128)} %bitcast.20, f32[2,128]{1,0:T(2,128)S(1)} %collective-permute-done.4.refs_3_, bf16[128,2048]{1,0:T(8,128)(2,1)} %refs_4_.1, ...), custom_call_target="tpu_custom_call" | custom-call | tf_op jit(solution)/shard_map/dispatch_scaled/pallas_call | solution.py:377
  17.0 8.6 %all-to-all-start.1 = ((bf16[16,48,1024]{2,1,0:T(8,128)(2,1)}), bf16[16,48,1024]{2,1,0:T(8,128)(2,1)S(1)}, u32[]{:S(2)}, u32[]{:S(2)}) async-start(bf16[16,48,1024]{2,1,0:T(8,128)(2,1)} %bitcast.24), calls=%async_computation.1 | async-start | bytes 3145728 | tf_op jit(solution)/shard_map/all_to_all | solution.py:335
  25.6 0.1 pad_add_fusion.place_ref
  25.7 14.3 %collective-permute-done.1.refs_3_ = bf16[128,2048]{1,0:T(8,128)(2,1)S(1)} collective-permute-done((bf16[128,2048]{1,0:T(8,128)(2,1)S(1)}, bf16[128,2048]{1,0:T(8,128)(2,1)S(1)}, u32[]{:S(2)}, u32[]{:S(2)}) %collective-permute-start.1) | collective-permute-done | bytes 524320 | tf_op jit(solution)/shard_map/ppermute | solution.py:330
  40.0 0.8 copy-done.5
  40.8 3.6 %dispatch_tokens.1 = (bf16[384,2048]{1,0:T(8,128)(2,1)}, s32[2,128]{1,0:T(2,128)S(1)}) custom-call(s32[2]{0:T(128)S(1)} %pad_add_fusion.place_ref, s32[2,128]{1,0:T(2,128)} %bitcast.33, s32[2,128]{1,0:T(2,128)S(1)} %collective-permute-done.refs_1_, bf16[128,2048]{1,0:T(8,128)(2,1)} %refs_2_.1, bf16[128,2048]{1,0:T(8,128)(2,1)} %copy-done.5), custom_call_target="tpu_custom_call" | custom-call | flops 30000001024 | bytes 30000000 | tf_op jit(solution)/shard_map/dispatch_tokens/pallas_call | solution.py:405
  44.4 22.7 %all-to-all-done.1 = bf16[16,48,1024]{2,1,0:T(8,128)(2,1)S(1)} async-done(((bf16[16,48,1024]{2,1,0:T(8,128)(2,1)}), bf16[16,48,1024]{2,1,0:T(8,128)(2,1)S(1)}, u32[]{:S(2)}, u32[]{:S(2)}) %all-to-all-start.1) | async-done | bytes 1572896 | tf_op jit(solution)/shard_map/all_to_all | solution.py:335
  67.1 4.0 %all-to-all-start = ((bf16[8,48,2048]{2,1,0:T(8,128)(2,1)}), bf16[8,48,2048]{2,1,0:T(8,128)(2,1)S(1)}, u32[]{:S(2)}, u32[]{:S(2)}) async-start(bf16[8,48,2048]{2,1,0:T(8,128)(2,1)} %bitcast.27), calls=%async_computation | async-start | bytes 3145728 | tf_op jit(solution)/shard_map/all_to_all | solution.py:335
  71.1 5.3 %back.1 = (f32[384,768]{1,0:T(8,128)}, bf16[384,768]{1,0:T(8,128)(2,1)}, bf16[768,1024]{1,0:T(8,128)(2,1)}) custom-call(s32[2]{0:T(128)S(1)} %pad_add_fusion.place_ref, bf16[768,1024]{1,0:T(8,128)(2,1)S(1)} %bitcast.18, bf16[768,1024]{1,0:T(8,128)(2,1)} %bitcast.28), custom_call_target="tpu_custom_call" | custom-call | tf_op jit(solution)/shard_map/back/pallas_call | solution.py:450
  76.4 0.2 collective-permute-start.6
  76.6 1.0 collective-permute-done.5.refs_0_
  77.5 1.4 ready.1
  78.9 10.4 %all-to-all-done = bf16[8,48,2048]{2,1,0:T(8,128)(2,1)S(1)} async-done(((bf16[8,48,2048]{2,1,0:T(8,128)(2,1)}), bf16[8,48,2048]{2,1,0:T(8,128)(2,1)S(1)}, u32[]{:S(2)}, u32[]{:S(2)}) %all-to-all-start) | async-done | bytes 1572896 | tf_op jit(solution)/shard_map/all_to_all | solution.py:335
  89.3 5.9 %forward.1 = (f32[384,768]{1,0:T(8,128)S(1)}, f32[384,768]{1,0:T(8,128)S(1)}, f32[384,768]{1,0:T(8,128)S(1)}, bf16[384,768]{1,0:T(8,128)(2,1)}, bf16[3,1024,768]...) custom-call(bf16[384,2048]{1,0:T(8,128)(2,1)S(1)} %bitcast.19, bf16[1024,768]{1,0:T(8,128)(2,1)S(1)} %get-tuple-element.34.gate_ref, ...), custom_call_target="tpu_custom_call" | custom-call | tf_op jit(solution)/shard_map/forward/pallas_call | solution.py:462
  95.2 4.8 %backward.1 = bf16[384,2176]{1,0:T(8,128)(2,1)} custom-call(s32[1]{0:T(128)} %bitcast.1.half_ref, f32[384,768]{1,0:T(8,128)S(1)} %get-tuple-element.41.act_ref, f32[384,768]{1,0:T(8,128)S(1)} %get-tuple-element.42.slope_ref, f32[384,768]{1,0:T(8,128)S(1)} %get-tuple-element.43.value_ref, bf16[1024,768]{1,0:T(8,128)(2,1)S(1)} %get-tuple-element.34.gate_ref, ...), custom_call_target="tpu_custom_call" | custom-call | tf_op jit(solution)/shard_map/backward/pallas_call | solution.py:482
  100.0 6.9 %all-to-all-start.2 = ((bf16[16,24,2176]{2,1,0:T(8,128)(2,1)}), bf16[16,24,2176]{2,1,0:T(8,128)(2,1)S(1)}, u32[]{:S(2)}, u32[]{:S(2)}) async-start(bf16[16,24,2176]{2,1,0:T(8,128)(2,1)} %bitcast.23), calls=%async_computation.2 | async-start | bytes 3342336 | tf_op jit(solution)/shard_map/all_to_all | solution.py:335
  106.9 0.2 collective-permute-start.7
  107.1 14.5 %collective-permute-done.7 = bf16[384,768]{1,0:T(8,128)(2,1)S(1)} collective-permute-done((bf16[384,768]{1,0:T(8,128)(2,1)}, bf16[384,768]{1,0:T(8,128)(2,1)S(1)}, u32[]{:S(2)}, u32[]{:S(2)}) %collective-permute-start.7) | collective-permute-done | bytes 589856 | tf_op jit(solution)/shard_map/ppermute | solution.py:326
  121.7 4.2 %convolution_bitcast_fusion = f32[1,768,1024]{2,1,0:T(8,128)} fusion(bf16[768,1024]{1,0:T(8,128)(2,1)S(1)} %copy-done.3, bf16[384,768]{1,0:T(8,128)(2,1)S(1)} %collective-permute-done.7, bf16[384,768]{1,0:T(8,128)(2,1)} %get-tuple-element.49), kind=kOutput, calls=%fused_computation | convolution fusion | flops 1210318848 | bytes 5898240 | tf_op jit(solution)/shard_map/dot_general | solution.py:23
  125.8 19.3 %all-to-all-done.2 = bf16[16,24,2176]{2,1,0:T(8,128)(2,1)S(1)} async-done(((bf16[16,24,2176]{2,1,0:T(8,128)(2,1)}), bf16[16,24,2176]{2,1,0:T(8,128)(2,1)S(1)}, u32[]{:S(2)}, u32[]{:S(2)}) %all-to-all-start.2) | async-done | bytes 1671200 | tf_op jit(solution)/shard_map/all_to_all | solution.py:335
  145.2 1.3 combine.1
  (13 shorter events, 0.0 us)
Async XLA Ops:
  1.6 9.8 %collective-permute-start.2 = (bf16[128,1024]{1,0:T(8,128)(2,1)S(1)}, bf16[128,1024]{1,0:T(8,128)(2,1)S(1)}, u32[]{:S(2)}, u32[]{:S(2)}) collective-permute-start(bf16[128,1024]{1,0:T(8,128)(2,1)S(1)} %constant_dynamic-slice_fusion), channel_id=1, source_target_pairs={{0,16},{16,0},{1,17},{17,1},{2,18},{18,2},{3,19},{19,3},{4,20},{20... | collective-permute-start | bytes 786440 | tf_op jit(solution)/shard_map/ppermute | solution.py:326
  2.9 5.2 %collective-permute-start = (s32[2,128]{1,0:T(2,128)}, s32[2,128]{1,0:T(2,128)S(1)}, u32[]{:S(2)}, u32[]{:S(2)}) collective-permute-start(s32[2,128]{1,0:T(2,128)} %bitcast.31), channel_id=1, source_target_pairs={{0,8},{1,9},{2,10},{3,11},{4,12},{5,13},{6,14},{7,15},{8,0},{9,1},... | collective-permute-start | bytes 3080 | tf_op jit(solution)/shard_map/ppermute | solution.py:330
  5.2 2.9 %copy-start.4 = (bf16[128,2048]{1,0:T(8,128)(2,1)S(1)}, bf16[128,2048]{1,0:T(8,128)(2,1)}, u32[]{:S(2)}) copy-start(bf16[128,2048]{1,0:T(8,128)(2,1)} %refs_2_.1) | copy-start | bytes 1572868
  5.2 3.5 %copy-start.2 = (s32[128,2]{0,1:T(2,128)S(1)}, s32[128,2]{0,1:T(2,128)}, u32[]{:S(2)}) copy-start(s32[128,2]{0,1:T(2,128)} %param.8) | copy-start | bytes 3076
  5.2 3.8 %copy-start = (f32[128,2]{0,1:T(2,128)S(1)}, f32[128,2]{0,1:T(2,128)}, u32[]{:S(2)}) copy-start(f32[128,2]{0,1:T(2,128)} %param.9) | copy-start | bytes 3076
  8.1 31.9 %collective-permute-start.1 = (bf16[128,2048]{1,0:T(8,128)(2,1)S(1)}, bf16[128,2048]{1,0:T(8,128)(2,1)S(1)}, u32[]{:S(2)}, u32[]{:S(2)}) collective-permute-start(bf16[128,2048]{1,0:T(8,128)(2,1)S(1)} %copy-done.4), channel_id=1, source_target_pairs={{0,8},{1,9},{2,10},{3,11},{4,12},{5,13},{6,14},{7,15},{8,0},{9,1},... | collective-permute-start | bytes 1572872 | tf_op jit(solution)/shard_map/ppermute | solution.py:330
  8.8 2.4 %collective-permute-start.3 = (s32[2,128]{1,0:T(2,128)S(1)}, s32[2,128]{1,0:T(2,128)S(1)}, u32[]{:S(2)}, u32[]{:S(2)}) collective-permute-start(s32[2,128]{1,0:T(2,128)S(1)} %bitcast.34), channel_id=1, source_target_pairs={{0,16},{16,0},{1,17},{17,1},{2,18},{18,2},{3,19},{19,3},{4,20},{20... | collective-permute-start | bytes 3080 | tf_op jit(solution)/shard_map/ppermute | solution.py:326
  9.0 2.4 %collective-permute-start.4 = (f32[2,128]{1,0:T(2,128)S(1)}, f32[2,128]{1,0:T(2,128)S(1)}, u32[]{:S(2)}, u32[]{:S(2)}) collective-permute-start(f32[2,128]{1,0:T(2,128)S(1)} %bitcast.21), channel_id=1, source_target_pairs={{0,16},{16,0},{1,17},{17,1},{2,18},{18,2},{3,19},{19,3},{4,20},{20... | collective-permute-start | bytes 3080 | tf_op jit(solution)/shard_map/ppermute | solution.py:326
  11.4 66.1 %collective-permute-start.5 = (bf16[2048,768]{1,0:T(8,128)(2,1)}, bf16[2048,768]{1,0:T(8,128)(2,1)}, u32[]{:S(2)}, u32[]{:S(2)}) collective-permute-start(bf16[2048,768]{1,0:T(8,128)(2,1)} %stack.10), channel_id=1, source_target_pairs={{0,16},{16,0},{1,17},{17,1},{2,18},{18,2},{3,19},{19,3},{4,20},{20... | collective-permute-start | bytes 9437192 | tf_op jit(solution)/shard_map/ppermute | solution.py:326
  17.0 50.1 %all-to-all-start.1 = ((bf16[16,48,1024]{2,1,0:T(8,128)(2,1)}), bf16[16,48,1024]{2,1,0:T(8,128)(2,1)S(1)}, u32[]{:S(2)}, u32[]{:S(2)}) async-start(bf16[16,48,1024]{2,1,0:T(8,128)(2,1)} %bitcast.24), calls=%async_computation.1 | async-start | bytes 3145728 | tf_op jit(solution)/shard_map/all_to_all | solution.py:335
  40.0 0.8 copy-start.5
  67.1 22.2 %all-to-all-start = ((bf16[8,48,2048]{2,1,0:T(8,128)(2,1)}), bf16[8,48,2048]{2,1,0:T(8,128)(2,1)S(1)}, u32[]{:S(2)}, u32[]{:S(2)}) async-start(bf16[8,48,2048]{2,1,0:T(8,128)(2,1)} %bitcast.27), calls=%async_computation | async-start | bytes 3145728 | tf_op jit(solution)/shard_map/all_to_all | solution.py:335
  76.4 18.8 %collective-permute-start.6 = (bf16[384,768]{1,0:T(8,128)(2,1)}, bf16[384,768]{1,0:T(8,128)(2,1)}, u32[]{:S(2)}, u32[]{:S(2)}) collective-permute-start(bf16[384,768]{1,0:T(8,128)(2,1)} %get-tuple-element.46), channel_id=1, source_target_pairs={{0,16},{16,0},{1,17},{17,1},{2,18},{18,2},{3,19},{19,3},{4,20},{20... | collective-permute-start | bytes 1769480 | tf_op jit(solution)/shard_map/ppermute | solution.py:326
  100.0 21.7 %copy-start.3 = (bf16[768,1024]{1,0:T(8,128)(2,1)S(1)}, bf16[768,1024]{1,0:T(8,128)(2,1)}, u32[]{:S(2)}) copy-start(bf16[768,1024]{1,0:T(8,128)(2,1)} %get-tuple-element.50) | copy-start | bytes 4718596
  100.0 45.2 %all-to-all-start.2 = ((bf16[16,24,2176]{2,1,0:T(8,128)(2,1)}), bf16[16,24,2176]{2,1,0:T(8,128)(2,1)S(1)}, u32[]{:S(2)}, u32[]{:S(2)}) async-start(bf16[16,24,2176]{2,1,0:T(8,128)(2,1)} %bitcast.23), calls=%async_computation.2 | async-start | bytes 3342336 | tf_op jit(solution)/shard_map/all_to_all | solution.py:335
  106.9 14.8 %collective-permute-start.7 = (bf16[384,768]{1,0:T(8,128)(2,1)}, bf16[384,768]{1,0:T(8,128)(2,1)S(1)}, u32[]{:S(2)}, u32[]{:S(2)}) collective-permute-start(bf16[384,768]{1,0:T(8,128)(2,1)} %get-tuple-element.49), channel_id=1, source_target_pairs={{0,16},{16,0},{1,17},{17,1},{2,18},{18,2},{3,19},{19,3},{4,20},{20... | collective-permute-start | bytes 1769480 | tf_op jit(solution)/shard_map/ppermute | solution.py:326
  121.7 23.5 %copy-start.1 = (f32[128,2]{0,1:T(2,128)S(1)}, f32[128,2]{0,1:T(2,128)}, u32[]{:S(2)}) copy-start(f32[128,2]{0,1:T(2,128)} %param.9) | copy-start | bytes 3076

commit v2 on v0

--- a/solution.py
+++ b/solution.py
@@ -204,7 +204,7 @@
         value_ref[:, cols] = hidden_f
         hidden_ref[:, cols] = hidden_f.astype(hidden_ref.dtype)
 
-    ahead = 2
+    ahead = 3
     for copies in stages[:ahead]:
         for copy in copies:
             copy.start()
@@ -341,6 +341,9 @@
             pltpu.VMEM((2 * share, hidden), jnp.bfloat16),
             pltpu.SemaphoreType.DMA((2, 8)),
         ],
+        cost_estimate=pl.CostEstimate(
+            flops=4 * 10**9, bytes_accessed=8 * share * hidden, transcendentals=0
+        ),
         compiler_params=params,
         name="stack",
     )(in_hbm(w_gate[0]), in_hbm(w_up[0]))

time: 147 us -> 146 us (level)
  starting transfers between devices: 28.2 us -> 25.7 us
  waiting for transfers between devices: 83.7 us -> 85.2 us
    all_to_all x3, starting transfers between devices: 20 us -> 17.9 us  [exchanged(): lax.all_to_all(split, 'expert', split_axis=0, concat_axis=0, axis_index_g...]
    all_to_all x3, waiting for transfers between devices: 38.8 us -> 40.6 us  [exchanged(): lax.all_to_all(split, 'expert', split_axis=0, concat_axis=0, axis_index_g...]
  transfers between devices with their start and end apart: 11 -> 11, of which waited for: 7 -> 7; matrix products, arithmetic and copies ran while one was open for 3% -> 4% of each run, Pallas kernels for 15% -> 15%
where the time goes in v2:
time: 146 us; the launch traced here: 145 us
  waiting for transfers between devices  85.2 us (58%)
  Pallas kernels  27.4 us (19%)
  starting transfers between devices  25.7 us (18%)
  matrix products  4.19 us (3%)
  local copies, waits for them, and re-layouts  1.77 us (1%)
    all_to_all x3, waiting for transfers between devices, exchanged(): lax.all_to_all(split, 'expert', split_axis=0, concat_axis=0, axis_index_g...  40.6 us
    ppermute x2, waiting for transfers between devices, across(): return lax.ppermute(value, 'expert', pairs)  24.8 us
    ppermute x6, waiting for transfers between devices, shifted(): lax.ppermute(value, 'dp', [(i, (i + by) % groups) for i in range(groups)])  19.7 us
    all_to_all x3, starting transfers between devices, exchanged(): lax.all_to_all(split, 'expert', split_axis=0, concat_axis=0, axis_index_g...  17.9 us
    pallas_call x1, Pallas kernels, per_device(): pl.pallas_call(functools.partial(forward_kernel, groups), out_shape=[pltp...  5.25 us
    pallas_call x1, Pallas kernels, per_device(): pl.pallas_call(functools.partial(back_kernel, groups, cap), out_shape=[pl...  5.22 us
    pallas_call x1, Pallas kernels, per_device(): pl.pallas_call(functools.partial(backward_kernel, groups, cap), out_shape...  4.74 us
    ppermute x6, starting transfers between devices, shifted(): lax.ppermute(value, 'dp', [(i, (i + by) % groups) for i in range(groups)])  4.5 us
  transfers between devices with their start and end apart: 11, of which 7 were waited for; matrix products, arithmetic and copies ran while one was open for 4% of the time, Pallas kernels for 15%

profile of v2, /device:TPU:11, one launch (start us, length us, event | category | flops | bytes accessed | tf_op | source)
XLA Modules:
  0.0 145.0 jit_solution(3950999107920841270)
XLA Ops:
  0.6 1.3 collective-permute-start.3
  1.9 2.3 %collective-permute-start = (s32[2,128]{1,0:T(2,128)}, s32[2,128]{1,0:T(2,128)S(1)}, u32[]{:S(2)}, u32[]{:S(2)}) collective-permute-start(s32[2,128]{1,0:T(2,128)} %bitcast.30), channel_id=1, source_target_pairs={{0,8},{1,9},{2,10},{3,11},{4,12},{5,13},{6,14},{7,15},{8,0},{9,1},... | collective-permute-start | bytes 3080 | tf_op jit(solution)/shard_map/ppermute | solution.py:312
  4.2 0.2 collective-permute-start.4
  4.5 1.0 constant_dynamic-slice_fusion
  5.4 1.3 collective-permute-start.2
  6.7 0.0 collective-permute-done.refs_1_
  6.7 1.0 collective-permute-start.1
  7.8 2.8 %stack.10 = bf16[2048,768]{1,0:T(8,128)(2,1)} custom-call(bf16[1024,768]{1,0:T(8,128)(2,1)} %bitcast.33, bf16[1024,768]{1,0:T(8,128)(2,1)} %bitcast.27), custom_call_target="tpu_custom_call" | custom-call | flops 4000000000 | bytes 6291456 | tf_op jit(solution)/shard_map/stack/pallas_call | solution.py:335
  10.6 0.0 collective-permute-done.4.refs_3_
  10.6 1.2 collective-permute-done.2.refs_5_
  11.8 1.2 collective-permute-start.5
  13.0 3.1 %dispatch_scaled.1 = bf16[768,1024]{1,0:T(8,128)(2,1)} custom-call(s32[1]{0:T(128)} %bitcast.place_ref, s32[2,128]{1,0:T(2,128)} %bitcast.31, s32[2,128]{1,0:T(2,128)S(1)} %collective-permute-done.3.refs_1_, f32[2,128]{1,0:T(2,128)} %bitcast.21, f32[2,128]{1,0:T(2,128)S(1)} %collective-permute-done.4.refs_3_, bf16[128,2048]{1,0:T(8,128)(2,1)} %refs_4_.1, ...), custom_call_target="tpu_custom_call" | custom-call | tf_op jit(solution)/shard_map/dispatch_scaled/pallas_call | solution.py:362
  16.2 6.6 %all-to-all-start.1 = ((bf16[16,48,1024]{2,1,0:T(8,128)(2,1)}), bf16[16,48,1024]{2,1,0:T(8,128)(2,1)S(1)}, u32[]{:S(2)}, u32[]{:S(2)}) async-start(bf16[16,48,1024]{2,1,0:T(8,128)(2,1)} %bitcast.24), calls=%async_computation.1 | async-start | bytes 3145728 | tf_op jit(solution)/shard_map/all_to_all | solution.py:317
  22.7 0.1 pad_add_fusion.place_ref
  22.8 24.8 %collective-permute-done.1.refs_3_ = bf16[128,2048]{1,0:T(8,128)(2,1)S(1)} collective-permute-done((bf16[128,2048]{1,0:T(8,128)(2,1)}, bf16[128,2048]{1,0:T(8,128)(2,1)S(1)}, u32[]{:S(2)}, u32[]{:S(2)}) %collective-permute-start.1) | collective-permute-done | bytes 524320 | tf_op jit(solution)/shard_map/ppermute | solution.py:312
  47.6 0.8 copy-done.2
  48.4 3.6 %dispatch_tokens.1 = (bf16[384,2048]{1,0:T(8,128)(2,1)}, s32[2,128]{1,0:T(2,128)S(1)}) custom-call(s32[2]{0:T(128)S(1)} %pad_add_fusion.place_ref, s32[2,128]{1,0:T(2,128)} %bitcast.32, s32[2,128]{1,0:T(2,128)S(1)} %collective-permute-done.refs_1_, bf16[128,2048]{1,0:T(8,128)(2,1)} %refs_2_.1, bf16[128,2048]{1,0:T(8,128)(2,1)} %copy-done.2), custom_call_target="tpu_custom_call" | custom-call | flops 30000001024 | bytes 30000000 | tf_op jit(solution)/shard_map/dispatch_tokens/pallas_call | solution.py:390
  52.0 13.9 %all-to-all-done.1 = bf16[16,48,1024]{2,1,0:T(8,128)(2,1)S(1)} async-done(((bf16[16,48,1024]{2,1,0:T(8,128)(2,1)}), bf16[16,48,1024]{2,1,0:T(8,128)(2,1)S(1)}, u32[]{:S(2)}, u32[]{:S(2)}) %all-to-all-start.1) | async-done | bytes 1572896 | tf_op jit(solution)/shard_map/all_to_all | solution.py:317
  65.9 4.0 %all-to-all-start = ((bf16[8,48,2048]{2,1,0:T(8,128)(2,1)}), bf16[8,48,2048]{2,1,0:T(8,128)(2,1)S(1)}, u32[]{:S(2)}, u32[]{:S(2)}) async-start(bf16[8,48,2048]{2,1,0:T(8,128)(2,1)} %bitcast.25), calls=%async_computation | async-start | bytes 3145728 | tf_op jit(solution)/shard_map/all_to_all | solution.py:317
  69.9 5.2 %back.1 = (f32[384,768]{1,0:T(8,128)}, bf16[384,768]{1,0:T(8,128)(2,1)}, bf16[768,1024]{1,0:T(8,128)(2,1)}) custom-call(s32[2]{0:T(128)S(1)} %pad_add_fusion.place_ref, bf16[768,1024]{1,0:T(8,128)(2,1)S(1)} %bitcast.18, bf16[768,1024]{1,0:T(8,128)(2,1)} %bitcast.26), custom_call_target="tpu_custom_call" | custom-call | tf_op jit(solution)/shard_map/back/pallas_call | solution.py:435
  75.1 0.2 collective-permute-start.6
  75.3 4.0 %collective-permute-done.5.refs_0_ = bf16[2048,768]{1,0:T(8,128)(2,1)} collective-permute-done((bf16[2048,768]{1,0:T(8,128)(2,1)}, bf16[2048,768]{1,0:T(8,128)(2,1)}, u32[]{:S(2)}, u32[]{:S(2)}) %collective-permute-start.5) | collective-permute-done | bytes 3145760 | tf_op jit(solution)/shard_map/ppermute | solution.py:308
  79.3 1.4 ready.1
  80.7 7.4 %all-to-all-done = bf16[8,48,2048]{2,1,0:T(8,128)(2,1)S(1)} async-done(((bf16[8,48,2048]{2,1,0:T(8,128)(2,1)}), bf16[8,48,2048]{2,1,0:T(8,128)(2,1)S(1)}, u32[]{:S(2)}, u32[]{:S(2)}) %all-to-all-start) | async-done | bytes 1572896 | tf_op jit(solution)/shard_map/all_to_all | solution.py:317
  88.1 5.3 %forward.1 = (f32[384,768]{1,0:T(8,128)S(1)}, f32[384,768]{1,0:T(8,128)S(1)}, f32[384,768]{1,0:T(8,128)S(1)}, bf16[384,768]{1,0:T(8,128)(2,1)}, bf16[3,1024,768]...) custom-call(bf16[384,2048]{1,0:T(8,128)(2,1)S(1)} %bitcast.19, bf16[1024,768]{1,0:T(8,128)(2,1)S(1)} %get-tuple-element.32.gate_ref, ...), custom_call_target="tpu_custom_call" | custom-call | tf_op jit(solution)/shard_map/forward/pallas_call | solution.py:447
  93.4 4.7 %backward.1 = bf16[384,2176]{1,0:T(8,128)(2,1)} custom-call(s32[1]{0:T(128)} %bitcast.1.half_ref, f32[384,768]{1,0:T(8,128)S(1)} %get-tuple-element.39.act_ref, f32[384,768]{1,0:T(8,128)S(1)} %get-tuple-element.40.slope_ref, f32[384,768]{1,0:T(8,128)S(1)} %get-tuple-element.41.value_ref, bf16[1024,768]{1,0:T(8,128)(2,1)S(1)} %get-tuple-element.32.gate_ref, ...), custom_call_target="tpu_custom_call" | custom-call | tf_op jit(solution)/shard_map/backward/pallas_call | solution.py:467
  98.1 7.3 %all-to-all-start.2 = ((bf16[16,24,2176]{2,1,0:T(8,128)(2,1)}), bf16[16,24,2176]{2,1,0:T(8,128)(2,1)S(1)}, u32[]{:S(2)}, u32[]{:S(2)}) async-start(bf16[16,24,2176]{2,1,0:T(8,128)(2,1)} %bitcast.23), calls=%async_computation.2 | async-start | bytes 3342336 | tf_op jit(solution)/shard_map/all_to_all | solution.py:317
  105.4 0.2 collective-permute-start.7
  105.7 14.5 %collective-permute-done.7 = bf16[384,768]{1,0:T(8,128)(2,1)S(1)} collective-permute-done((bf16[384,768]{1,0:T(8,128)(2,1)}, bf16[384,768]{1,0:T(8,128)(2,1)S(1)}, u32[]{:S(2)}, u32[]{:S(2)}) %collective-permute-start.7) | collective-permute-done | bytes 589856 | tf_op jit(solution)/shard_map/ppermute | solution.py:308
  120.2 4.2 %convolution_bitcast_fusion = f32[1,768,1024]{2,1,0:T(8,128)} fusion(bf16[768,1024]{1,0:T(8,128)(2,1)S(1)} %copy-done.1, bf16[384,768]{1,0:T(8,128)(2,1)S(1)} %collective-permute-done.7, bf16[384,768]{1,0:T(8,128)(2,1)} %get-tuple-element.47), kind=kOutput, calls=%fused_computation | convolution fusion | flops 1210318848 | bytes 5898240 | tf_op jit(solution)/shard_map/dot_general | solution.py:23
  124.4 19.3 %all-to-all-done.2 = bf16[16,24,2176]{2,1,0:T(8,128)(2,1)S(1)} async-done(((bf16[16,24,2176]{2,1,0:T(8,128)(2,1)}), bf16[16,24,2176]{2,1,0:T(8,128)(2,1)S(1)}, u32[]{:S(2)}, u32[]{:S(2)}) %all-to-all-start.2) | async-done | bytes 1671200 | tf_op jit(solution)/shard_map/all_to_all | solution.py:317
  143.7 1.3 combine.1
  (7 shorter events, 0.0 us)
Async XLA Ops:
  0.6 9.9 %collective-permute-start.3 = (s32[2,128]{1,0:T(2,128)}, s32[2,128]{1,0:T(2,128)S(1)}, u32[]{:S(2)}, u32[]{:S(2)}) collective-permute-start(s32[2,128]{1,0:T(2,128)} %bitcast.29), channel_id=1, source_target_pairs={{0,16},{16,0},{1,17},{17,1},{2,18},{18,2},{3,19},{19,3},{4,20},{20... | collective-permute-start | bytes 3080 | tf_op jit(solution)/shard_map/ppermute | solution.py:308
  1.9 4.8 %collective-permute-start = (s32[2,128]{1,0:T(2,128)}, s32[2,128]{1,0:T(2,128)S(1)}, u32[]{:S(2)}, u32[]{:S(2)}) collective-permute-start(s32[2,128]{1,0:T(2,128)} %bitcast.30), channel_id=1, source_target_pairs={{0,8},{1,9},{2,10},{3,11},{4,12},{5,13},{6,14},{7,15},{8,0},{9,1},... | collective-permute-start | bytes 3080 | tf_op jit(solution)/shard_map/ppermute | solution.py:312
  4.2 6.3 %collective-permute-start.4 = (f32[2,128]{1,0:T(2,128)}, f32[2,128]{1,0:T(2,128)S(1)}, u32[]{:S(2)}, u32[]{:S(2)}) collective-permute-start(f32[2,128]{1,0:T(2,128)} %bitcast.20), channel_id=1, source_target_pairs={{0,16},{16,0},{1,17},{17,1},{2,18},{18,2},{3,19},{19,3},{4,20},{20... | collective-permute-start | bytes 3080 | tf_op jit(solution)/shard_map/ppermute | solution.py:308
  5.4 6.4 %collective-permute-start.2 = (bf16[128,1024]{1,0:T(8,128)(2,1)S(1)}, bf16[128,1024]{1,0:T(8,128)(2,1)S(1)}, u32[]{:S(2)}, u32[]{:S(2)}) collective-permute-start(bf16[128,1024]{1,0:T(8,128)(2,1)S(1)} %constant_dynamic-slice_fusion), channel_id=1, source_target_pairs={{0,16},{16,0},{1,17},{17,1},{2,18},{18,2},{3,19},{19,3},{4,20},{20... | collective-permute-start | bytes 786440 | tf_op jit(solution)/shard_map/ppermute | solution.py:308
  6.7 40.9 %collective-permute-start.1 = (bf16[128,2048]{1,0:T(8,128)(2,1)}, bf16[128,2048]{1,0:T(8,128)(2,1)S(1)}, u32[]{:S(2)}, u32[]{:S(2)}) collective-permute-start(bf16[128,2048]{1,0:T(8,128)(2,1)} %refs_2_.1), channel_id=1, source_target_pairs={{0,8},{1,9},{2,10},{3,11},{4,12},{5,13},{6,14},{7,15},{8,0},{9,1},... | collective-permute-start | bytes 1572872 | tf_op jit(solution)/shard_map/ppermute | solution.py:312
  11.8 67.5 %collective-permute-start.5 = (bf16[2048,768]{1,0:T(8,128)(2,1)}, bf16[2048,768]{1,0:T(8,128)(2,1)}, u32[]{:S(2)}, u32[]{:S(2)}) collective-permute-start(bf16[2048,768]{1,0:T(8,128)(2,1)} %stack.10), channel_id=1, source_target_pairs={{0,16},{16,0},{1,17},{17,1},{2,18},{18,2},{3,19},{19,3},{4,20},{20... | collective-permute-start | bytes 9437192 | tf_op jit(solution)/shard_map/ppermute | solution.py:308
  16.2 49.8 %all-to-all-start.1 = ((bf16[16,48,1024]{2,1,0:T(8,128)(2,1)}), bf16[16,48,1024]{2,1,0:T(8,128)(2,1)S(1)}, u32[]{:S(2)}, u32[]{:S(2)}) async-start(bf16[16,48,1024]{2,1,0:T(8,128)(2,1)} %bitcast.24), calls=%async_computation.1 | async-start | bytes 3145728 | tf_op jit(solution)/shard_map/all_to_all | solution.py:317
  47.6 0.8 copy-start.2
  65.9 22.2 %all-to-all-start = ((bf16[8,48,2048]{2,1,0:T(8,128)(2,1)}), bf16[8,48,2048]{2,1,0:T(8,128)(2,1)S(1)}, u32[]{:S(2)}, u32[]{:S(2)}) async-start(bf16[8,48,2048]{2,1,0:T(8,128)(2,1)} %bitcast.25), calls=%async_computation | async-start | bytes 3145728 | tf_op jit(solution)/shard_map/all_to_all | solution.py:317
  75.1 18.3 %collective-permute-start.6 = (bf16[384,768]{1,0:T(8,128)(2,1)}, bf16[384,768]{1,0:T(8,128)(2,1)}, u32[]{:S(2)}, u32[]{:S(2)}) collective-permute-start(bf16[384,768]{1,0:T(8,128)(2,1)} %get-tuple-element.44), channel_id=1, source_target_pairs={{0,16},{16,0},{1,17},{17,1},{2,18},{18,2},{3,19},{19,3},{4,20},{20... | collective-permute-start | bytes 1769480 | tf_op jit(solution)/shard_map/ppermute | solution.py:308
  98.1 22.1 %copy-start.1 = (bf16[768,1024]{1,0:T(8,128)(2,1)S(1)}, bf16[768,1024]{1,0:T(8,128)(2,1)}, u32[]{:S(2)}) copy-start(bf16[768,1024]{1,0:T(8,128)(2,1)} %get-tuple-element.48) | copy-start | bytes 4718596
  98.1 45.6 %all-to-all-start.2 = ((bf16[16,24,2176]{2,1,0:T(8,128)(2,1)}), bf16[16,24,2176]{2,1,0:T(8,128)(2,1)S(1)}, u32[]{:S(2)}, u32[]{:S(2)}) async-start(bf16[16,24,2176]{2,1,0:T(8,128)(2,1)} %bitcast.23), calls=%async_computation.2 | async-start | bytes 3342336 | tf_op jit(solution)/shard_map/all_to_all | solution.py:317
  105.4 14.8 %collective-permute-start.7 = (bf16[384,768]{1,0:T(8,128)(2,1)}, bf16[384,768]{1,0:T(8,128)(2,1)S(1)}, u32[]{:S(2)}, u32[]{:S(2)}) collective-permute-start(bf16[384,768]{1,0:T(8,128)(2,1)} %get-tuple-element.47), channel_id=1, source_target_pairs={{0,16},{16,0},{1,17},{17,1},{2,18},{18,2},{3,19},{19,3},{4,20},{20... | collective-permute-start | bytes 1769480 | tf_op jit(solution)/shard_map/ppermute | solution.py:308
  120.2 23.5 %copy-start = (f32[128,2]{0,1:T(2,128)S(1)}, f32[128,2]{0,1:T(2,128)}, u32[]{:S(2)}) copy-start(f32[128,2]{0,1:T(2,128)} %param.9) | copy-start | bytes 3076
